TPU v7x, 32 devices: a whole 2x2x4 slice. The times are simulated.
32 devices in a mesh: rep: 2 (over y), dp: 4 (over z), tp: 4 (over x, core).
Axes of the slice: x: 2, y: 2, z: 4, core: 2. Of those that a mesh axis runs over, the one named last changes fastest.
Arguments:
- attention_input: bfloat16 [2048, 8192], P(('rep', 'dp'), 'tp'), parts along dimension 0, may hold values from -6 to 6
- output_weight: bfloat16 [8192, 4096], P('tp'), may hold values from -0.09375 to 0.09375
- adapter_down_weight: bfloat16 [16, 8192, 64], P('dp', 'tp'), may hold values from -0.0625 to 0.0625
- adapter_up_weight: bfloat16 [16, 64, 4096], P('dp', None, 'tp'), may hold values from -0.75 to 0.75
- fetched_local_numbers: int32 [8, 4, 2], P('rep'), parts along dimension 0, may hold values from 0 to 3, as said below
- request_adapter_entry: int32 [2048], P(('rep', 'dp')), parts along dimension 0, may hold values from 0 to 7, as said below
Outputs:
- projected: bfloat16 [2048, 4096], P(('rep', 'dp'), 'tp'), parts along dimension 0
There are 2 independent parts, one for each index of `rep`. A program takes and returns all parts, laid end to end along the dimension named above; an argument that names none is the same for every part. Nothing has to cross between parts.
Inputs may be any that keep to these rules, and one draw needn't show every extreme that they name: `fetched_local_numbers`: for each g and o the 2 entries are different local numbers. `request_adapter_entry`: among the 256 requests of one index of dp at most 128 name one owner, and one owner is named exactly 128 times.
All inputs are finite; a program needn't handle non-finite values.
Results may differ from a plain program's by a relative error of at most 0.001.
Values may be sent and summed in bfloat16 or wider, within the bound.
A program may use at most 64 MiB of HBM per device.

v0:
```python
import jax
import jax.numpy as jnp
from jax import lax
from jax.sharding import PartitionSpec as P

adapter_scale = 0.5


def body(
    attention_input,
    output_weight,
    adapter_down_weight,
    adapter_up_weight,
    fetched_local_numbers,
    request_adapter_entry,
):
    request_batch = attention_input.shape[0]
    groups = lax.axis_size("dp")
    myself = lax.axis_index("dp")
    capacity = fetched_local_numbers.shape[2]
    adapter_rank_width = adapter_down_weight.shape[2]
    local_output_rows = adapter_up_weight.shape[2]
    partial_value = jnp.dot(attention_input, output_weight, preferred_element_type=jnp.float32)
    local_base_weight = lax.psum_scatter(partial_value, "tp", scatter_dimension=1, tiled=True)
    owner_source = lax.dynamic_index_in_dim(fetched_local_numbers, myself, 1, keepdims=False)
    outgoing_down = jnp.take(adapter_down_weight, owner_source, axis=0)
    outgoing_up = jnp.take(adapter_up_weight, owner_source, axis=0)
    received_down, received_up = (
        lax.all_to_all(outgoing_down, "dp", split_axis=0, concat_axis=0, tiled=True),
        lax.all_to_all(outgoing_up, "dp", split_axis=0, concat_axis=0, tiled=True),
    )
    entry_count = groups * capacity
    entry_onehot = (
        request_adapter_entry[:, None] == jnp.arange(entry_count, dtype=jnp.int32)[None, :]
    ).astype(jnp.float32)
    products = jnp.einsum(
        "nh,shr->nsr",
        attention_input,
        received_down.reshape(entry_count, -1, adapter_rank_width),
        preferred_element_type=jnp.float32,
    )
    shrunk_part = jnp.sum(products * entry_onehot[:, :, None], axis=1)
    reduced_activation = lax.psum(shrunk_part, "tp")
    expanded_rows = (entry_onehot[:, :, None] * reduced_activation[:, None, :]).reshape(
        request_batch, entry_count * adapter_rank_width
    )
    adapter_correction = jnp.dot(
        expanded_rows,
        received_up.reshape(entry_count * adapter_rank_width, local_output_rows).astype(
            jnp.float32
        ),
        precision=lax.Precision.HIGHEST,
    )
    return (local_base_weight + adapter_scale * adapter_correction).astype(jnp.bfloat16)


def solution(mesh):
    in_specs = (
        P(("rep", "dp"), "tp"),
        P("tp", None),
        P("dp", "tp", None),
        P("dp", None, "tp"),
        P("rep", None, None),
        P(("rep", "dp")),
    )
    out_specs = P(("rep", "dp"), "tp")
    return jax.shard_map(body, mesh=mesh, in_specs=in_specs, out_specs=out_specs, check_vma=False)
```

profile of v0, /device:TPU:0, one launch (start us, length us, event | category | flops | bytes accessed | tf_op | source)
XLA Modules:
  0.0 154.8 jit_solution(12126212228324712795)
XLA Ops:
  6.5 0.0 copy-start
  6.5 0.8 constant_dynamic-slice_fusion
  7.4 0.1 copy.12
  7.5 0.1 copy.15
  7.6 0.1 reshape.80
  7.7 0.1 copy.13
  7.8 1.9 %gather_fusion = bf16[8,2048,64]{1,2,0:T(8,128)(2,1)S(1)} fusion(bf16[4,2048,64]{1,2,0:T(8,128)(2,1)} %param.8, s32[1024]{0:T(1024)S(1)} %pad_clamp_fusion), kind=kCustom, calls=%fused_computation | custom fusion | bytes 4194336 | tf_op jit(solution)/shard_map/jit(_take)/gather | solution.py:26
  9.7 1.6 %broadcast_select_fusion = bf16[4,2,2048,64]{2,3,1,0:T(8,128)(2,1)} fusion(bf16[4,2,2048,64]{2,3,1,0:T(8,128)(2,1)S(1)} %bitcast.25, pred[4,2]{1,0:T(4,128)(4,1)S(1)} %copy.13), kind=kLoop, calls=%fused_computation.2 | loop fusion | flops 1048576 | bytes 4194312 | tf_op jit(solution)/shard_map/jit(_take)/select_n | solution.py:26
  11.3 0.0 copy-start.2
  11.3 6.4 %all-to-all-start = ((bf16[4,2,2048,64]{2,3,1,0:T(8,128)(2,1)}), bf16[4,2,2048,64]{2,3,1,0:T(8,128)(2,1)S(1)}, u32[]{:S(2)}, u32[]{:S(2)}) async-start(bf16[4,2,2048,64]{2,3,1,0:T(8,128)(2,1)} %broadcast_select_fusion), calls=%async_computation.1 | async-start | bytes 4194304 | tf_op jit(solution)/shard_map/all_to_all | solution.py:29
  17.8 0.0 all-reduce.2.cloned.1.call-start
  17.8 0.0 copy-done.2
  17.8 48.2 %all-to-all-done = bf16[4,2,2048,64]{2,3,1,0:T(8,128)(2,1)S(1)} async-done(((bf16[4,2,2048,64]{2,3,1,0:T(8,128)(2,1)}), bf16[4,2,2048,64]{2,3,1,0:T(8,128)(2,1)S(1)}, u32[]{:S(2)}, u32[]{:S(2)}) %all-to-all-start) | async-done | bytes 2097184 | tf_op jit(solution)/shard_map/all_to_all | solution.py:29
  66.0 0.0 copy-done
  66.0 1.4 fusion.3
  67.3 0.0 all-reduce.2.cloned.1.call-update
  67.4 0.0 reduce-scatter.2.cloned.1.call-start
  67.4 10.1 %fusion.6 = f32[256,4096]{1,0:T(8,128)} fusion(bf16[256,2048]{1,0:T(8,128)(2,1)S(1)} %copy-done, bf16[2048,4096]{1,0:T(8,128)(2,1)} %param.7), kind=kOutput, calls=%fused_computation.19 | convolution fusion | flops 4294967296 | bytes 22020096 | tf_op jit(solution)/shard_map/dot_general | solution.py:23
  77.5 0.0 copy-start.1
  77.5 0.0 reduce-scatter.2.cloned.1.call-update
  77.5 1.0 copy-done.1
  78.6 0.6 gather_fusion.1
  79.2 1.2 broadcast_select_fusion.1
  80.3 3.5 %all-to-all-start.1 = ((bf16[4,2,64,1024]{3,2,1,0:T(8,128)(2,1)}), bf16[4,2,64,1024]{3,2,1,0:T(8,128)(2,1)S(1)}, u32[]{:S(2)}, u32[]{:S(2)}) async-start(bf16[4,2,64,1024]{3,2,1,0:T(8,128)(2,1)} %broadcast_select_fusion.1), calls=%async_computation.2 | async-start | bytes 2097152 | tf_op jit(solution)/shard_map/all_to_all | solution.py:30
  83.9 13.8 %all-reduce.2.cloned.1.call-done = f32[256,64]{0,1:T(8,128)} async-done(((f32[256,64]{0,1:T(8,128)}), f32[256,64]{0,1:T(8,128)}) %all-reduce.2.cloned.1.call-update) | async-done | bytes 65552 | tf_op jit(solution)/shard_map/psum | solution.py:43
  97.7 0.9 broadcast_multiply_fusion
  98.6 10.4 %all-to-all-done.1 = bf16[4,2,64,1024]{3,2,1,0:T(8,128)(2,1)S(1)} async-done(((bf16[4,2,64,1024]{3,2,1,0:T(8,128)(2,1)}), bf16[4,2,64,1024]{3,2,1,0:T(8,128)(2,1)S(1)}, u32[]{:S(2)}, u32[]{:S(2)}) %all-to-all-start.1) | async-done | bytes 1048608 | tf_op jit(solution)/shard_map/all_to_all | solution.py:30
  109.0 35.9 %reduce-scatter.2.cloned.1.call-done = f32[256,1024]{1,0:T(8,128)} async-done(((f32[256,4096]{1,0:T(8,128)}), f32[256,1024]{1,0:T(8,128)}) %reduce-scatter.2.cloned.1.call-update) | async-done | bytes 1048592 | tf_op jit(solution)/shard_map/reduce_scatter | solution.py:24
  144.9 3.0 %fusion.1 = bf16[256,1024]{1,0:T(8,128)(2,1)} fusion(f32[256,1024]{1,0:T(8,128)} %reduce-scatter.2.cloned.1.call-done, f32[256,512]{0,1:T(8,128)S(1)} %bitcast.29, bf16[512,1024]{1,0:T(8,128)(2,1)S(1)} %bitcast.26), kind=kOutput, calls=%fused_computation.5 | convolution fusion | flops 1611399168 | bytes 3145728 | tf_op jit(solution)/shard_map/dot_general | solution.py:47
  (4 shorter events, 0.0 us)
Async XLA Ops:
  6.5 59.4 %copy-start = (bf16[256,2048]{1,0:T(8,128)(2,1)S(1)}, bf16[256,2048]{1,0:T(8,128)(2,1)}, u32[]{:S(2)}) copy-start(bf16[256,2048]{1,0:T(8,128)(2,1)} %param.6) | copy-start | bytes 3145732
  11.3 6.5 %copy-start.2 = (s32[256]{0:T(256)S(1)}, s32[256]{0:T(256)}, u32[]{:S(2)}) copy-start(s32[256]{0:T(256)} %param.11) | copy-start | bytes 3076
  11.3 54.6 %all-to-all-start = ((bf16[4,2,2048,64]{2,3,1,0:T(8,128)(2,1)}), bf16[4,2,2048,64]{2,3,1,0:T(8,128)(2,1)S(1)}, u32[]{:S(2)}, u32[]{:S(2)}) async-start(bf16[4,2,2048,64]{2,3,1,0:T(8,128)(2,1)} %broadcast_select_fusion), calls=%async_computation.1 | async-start | bytes 4194304 | tf_op jit(solution)/shard_map/all_to_all | solution.py:29
  17.8 80.0 %all-reduce.2.cloned.1.call-start = ((), (), s32[]{:S(2)}) async-start(), calls=%async_computation.4 | async-start | bytes 131072 | tf_op jit(solution)/shard_map/psum | solution.py:43
  67.4 77.6 %reduce-scatter.2.cloned.1.call-start = ((), (), s32[]{:S(2)}) async-start(), calls=%async_computation.3 | async-start | bytes 5242880 | tf_op jit(solution)/shard_map/reduce_scatter | solution.py:24
  77.5 1.0 copy-start.1
  80.3 28.7 %all-to-all-start.1 = ((bf16[4,2,64,1024]{3,2,1,0:T(8,128)(2,1)}), bf16[4,2,64,1024]{3,2,1,0:T(8,128)(2,1)S(1)}, u32[]{:S(2)}, u32[]{:S(2)}) async-start(bf16[4,2,64,1024]{3,2,1,0:T(8,128)(2,1)} %broadcast_select_fusion.1), calls=%async_computation.2 | async-start | bytes 2097152 | tf_op jit(solution)/shard_map/all_to_all | solution.py:30
Sparse Core Ops, SparseCore 0:
  67.5 30.1 all-reduce.1
  100.4 44.4 reduce-scatter.1
where the time goes:
time: 155 us
  waiting for transfers between devices  108 us (70%)
  matrix products  14.5 us (9%)
  between operations  13.4 us (9%)
  starting transfers between devices  10 us (6%)
  local copies, waits for them, and re-layouts  4.78 us (3%)
  other arithmetic  3.67 us (2%)
    all_to_all x1, waiting for transfers between devices, body(): lax.all_to_all(outgoing_down, 'dp', split_axis=0, concat_axis=0, tiled=True)  48.2 us
    reduce_scatter x1, waiting for transfers between devices, body(): lax.psum_scatter(partial_value, 'tp', scatter_dimension=1, tiled=True)  35.9 us
    psum x1, waiting for transfers between devices, body(): reduced_activation = lax.psum(shrunk_part, 'tp')  13.8 us
    all_to_all x1, waiting for transfers between devices, body(): lax.all_to_all(outgoing_up, 'dp', split_axis=0, concat_axis=0, tiled=True)  10.4 us
    dot_general x1, matrix products, body(): jnp.dot(attention_input, output_weight, preferred_element_type=jnp.float32)  10.1 us
    all_to_all x1, starting transfers between devices, body(): lax.all_to_all(outgoing_down, 'dp', split_axis=0, concat_axis=0, tiled=True)  6.45 us
    all_to_all x1, starting transfers between devices, body(): lax.all_to_all(outgoing_up, 'dp', split_axis=0, concat_axis=0, tiled=True)  3.51 us
  transfers between devices with their start and end apart: 4, of which 4 were waited for; matrix products, arithmetic and copies ran while one was open for 8% of the time, Pallas kernels for 0%

commit v1 on v0

v1 whole, which is shorter than its diff:
```python
import functools

import jax
import jax.numpy as jnp
from jax import lax
from jax.experimental import pallas as pl
from jax.experimental.pallas import tpu as pltpu
from jax.sharding import PartitionSpec as P

adapter_scale = 0.5
CORES = 2


def kernel(
    sizes,
    entry_ref,
    fetched_ref,
    x_hbm,
    w_hbm,
    down_hbm,
    up_hbm,
    out_ref,
    x,
    w,
    downs,
    ups,
    part,
    core_in,
    x_in,
    shr,
    shr_in,
    aid,
    local_sem,
    w_sem,
    core_sem,
    xs_sem,
    shr_sem,
    zd_sem,
    yd_sem,
    zu_sem,
    yu_sem,
):
    reps, groups, tps, rank = sizes
    chips = tps // CORES
    rep = lax.axis_index("rep")
    me = lax.axis_index("dp")
    tp = lax.axis_index("tp")
    core = lax.rem(tp, CORES)
    chip = lax.div(tp, CORES)
    other_core = CORES * chip + (1 - core)
    other_rep = 1 - rep
    rows = x.shape[0]
    width = out_ref.shape[1]
    held = downs.shape[2]
    half = held // rank
    stored = half * reps
    cap = fetched_ref.shape[2]
    tile = w.shape[3]
    tiles = w.shape[1]
    f32 = jnp.float32

    def remote(src, dst, send, recv, target):
        return pltpu.make_async_remote_copy(
            src_ref=src,
            dst_ref=dst,
            send_sem=send,
            recv_sem=recv,
            device_id=target,
            device_id_type=pl.DeviceIdType.MESH,
        )

    load_x = pltpu.make_async_copy(x_hbm, x, local_sem.at[0])
    load_down = pltpu.make_async_copy(down_hbm, downs.at[me], local_sem.at[1])
    load_up = pltpu.make_async_copy(up_hbm, ups.at[me], local_sem.at[2])
    load_x.start()

    def column_of(j):
        far = lax.rem(chip + lax.div(j, 2) + 1, chips)
        return CORES * far + jnp.where(lax.rem(j, 2) == 0, 1 - core, core)

    def load_w(j, n):
        start = pl.multiple_of(column_of(j) * width + n * tile, 128)
        return pltpu.make_async_copy(
            w_hbm.at[:, pl.ds(start, tile)], w.at[j, n], w_sem.at[j, n]
        )

    @pl.loop(0, tps)
    def _(j):
        for n in range(tiles):
            load_w(j, n).start()

    load_down.start()
    load_up.start()

    barrier = pltpu.get_barrier_semaphore()

    def greet(target):
        pl.semaphore_signal(
            barrier, inc=1, device_id=target, device_id_type=pl.DeviceIdType.MESH
        )

    @pl.when(me > 0)
    def _():
        greet({"dp": me - 1})

    @pl.when(me < groups - 1)
    def _():
        greet({"dp": me + 1})

    greet({"rep": other_rep})

    @pl.loop(1, tps)
    def _(q):
        greet({"tp": lax.rem(tp + q, tps)})

    ends = jnp.where(me > 0, 1, 0) + jnp.where(me < groups - 1, 1, 0)
    pl.semaphore_wait(barrier, tps + ends)

    down_kind = (downs, down_hbm, zd_sem, yd_sem)
    up_kind = (ups, up_hbm, zu_sem, yu_sem)

    def piece(a):
        return pl.ds(a * rank, rank)

    def z_copy(kind, owner, a, side, own=False):
        buffer, source, z, _ = kind
        src = source.at[rep, piece(a)] if own else buffer.at[owner, rep, piece(a)]
        target = {"dp": me - 1} if side == 0 else {"dp": me + 1}
        return remote(
            src, buffer.at[owner, rep, piece(a)], z.at[side, owner, a], z.at[2, owner, a], target
        )

    def y_copy(kind, owner, a, mine):
        buffer, _, _, y = kind
        place = buffer.at[owner, rep if mine else other_rep, piece(a)]
        return remote(place, place, y.at[0, owner, a], y.at[1, owner, a], {"rep": other_rep})

    def send_own(kind, act):
        for a in range(half):

            @pl.when(me > 0)
            def _():
                act(z_copy(kind, me, a, 0, True))

            @pl.when(me < groups - 1)
            def _():
                act(z_copy(kind, me, a, 1, True))

    def relay(kind, k, a):
        @pl.when(me - k >= 0)
        def _():
            z_copy(kind, me - k, a, 1).wait_recv()

            @pl.when(me < groups - 1)
            def _():
                z_copy(kind, me - k, a, 1).start()

            y_copy(kind, me - k, a, True).start()

        @pl.when(me + k < groups)
        def _():
            z_copy(kind, me + k, a, 0).wait_recv()

            @pl.when(me > 0)
            def _():
                z_copy(kind, me + k, a, 0).start()

            y_copy(kind, me + k, a, True).start()

    def settle(kind, k, a):
        @pl.when(me - k >= 0)
        def _():
            @pl.when(me < groups - 1)
            def _():
                z_copy(kind, me - k, a, 1).wait_send()

            y_copy(kind, me - k, a, True).wait_send()

        @pl.when(me + k < groups)
        def _():
            @pl.when(me > 0)
            def _():
                z_copy(kind, me + k, a, 0).wait_send()

            y_copy(kind, me + k, a, True).wait_send()

    send_own(down_kind, lambda c: c.start())

    def core_copy(s):
        return remote(
            part.at[2 * s], core_in.at[s], core_sem.at[0, s], core_sem.at[1, s], {"tp": other_core}
        )

    def chip_copy(s):
        far = lax.rem(chip + s + 1, chips)
        return remote(
            part.at[2 * s + 1],
            x_in.at[s],
            xs_sem.at[0, s],
            xs_sem.at[1, s],
            {"tp": CORES * far + core},
        )

    load_x.wait()

    def multiply(j):
        @pl.loop(0, tiles)
        def _(n):
            load_w(j, n).wait()
            part[j, :, pl.ds(pl.multiple_of(n * tile, 128), tile)] = jnp.dot(
                x[...], w[j, n], preferred_element_type=f32
            )

    @pl.loop(0, chips)
    def _(s):
        multiply(2 * s)
        core_copy(s).start()

        @pl.when(s > 0)
        def _():
            core_copy(s - 1).wait_recv()
            part[2 * s - 1] = part[2 * s - 1] + core_in[s - 1]
            chip_copy(s - 1).start()

        multiply(2 * s + 1)

    aid[...] = jnp.zeros_like(aid)

    @pl.loop(0, groups)
    def _(o):
        entry = entry_ref[...]
        number = aid[...]
        for e in range(cap):
            number = jnp.where(entry == cap * o + e, stored * o + fetched_ref[me, o, e], number)
        aid[...] = number

    lane = lax.broadcasted_iota(jnp.int32, (rows, held), 1)
    lane_adapter = lax.div(lane, rank)

    def chosen(o, h):
        return aid[...] == stored * o + half * h + lane_adapter

    def shrink(o, h):
        product = lax.dot_general(
            x[...], downs[o, h], (((1,), (1,)), ((), ())), preferred_element_type=f32
        )
        shr[...] += jnp.where(chosen(o, h), product, 0.0)

    shr[...] = jnp.zeros_like(shr)
    load_down.wait()

    @pl.loop(0, reps)
    def _(h):
        shrink(me, h)

    @pl.loop(1, groups)
    def _(k):
        for a in range(half):
            relay(down_kind, k, a)

        @pl.when(me - k >= 0)
        def _():
            shrink(me - k, rep)

        @pl.when(me + k < groups)
        def _():
            shrink(me + k, rep)

    send_own(up_kind, lambda c: c.start())

    @pl.loop(0, groups)
    def _(o):
        @pl.when(o != me)
        def _():
            for a in range(half):
                y_copy(down_kind, o, a, False).wait_recv()
            shrink(o, other_rep)

    def shr_copy(q):
        return remote(
            shr,
            shr_in.at[q - 1],
            shr_sem.at[0, q - 1],
            shr_sem.at[1, q - 1],
            {"tp": lax.rem(tp + q, tps)},
        )

    @pl.loop(1, tps)
    def _(q):
        shr_copy(q).start()

    @pl.loop(1, groups)
    def _(k):
        for a in range(half):
            relay(up_kind, k, a)

    @pl.loop(1, tps)
    def _(q):
        shr_copy(q).wait()

    @pl.loop(1, tps)
    def _(q):
        shr[...] += shr_in[q - 1]

    base = part.at[tps - 1]
    core_copy(chips - 1).wait_recv()
    base[...] += core_in[chips - 1]

    @pl.loop(0, chips - 1)
    def _(s):
        chip_copy(s).wait_recv()
        base[...] += x_in[s]

    def expand(o, h):
        factor = jnp.where(chosen(o, h), adapter_scale * shr[...], 0.0)
        high = factor.astype(jnp.bfloat16)
        low = (factor - high.astype(f32)).astype(jnp.bfloat16)
        up = ups[o, h]
        base[...] += jnp.dot(high, up, preferred_element_type=f32) + jnp.dot(
            low, up, preferred_element_type=f32
        )

    load_up.wait()
    expand(me, other_rep)

    @pl.loop(0, groups)
    def _(o):
        expand(o, rep)

    @pl.loop(0, groups)
    def _(o):
        @pl.when(o != me)
        def _():
            for a in range(half):
                y_copy(up_kind, o, a, False).wait_recv()
            expand(o, other_rep)

    out_ref[...] = base[...].astype(out_ref.dtype)

    @pl.loop(0, chips)
    def _(s):
        core_copy(s).wait_send()

    @pl.loop(0, chips - 1)
    def _(s):
        chip_copy(s).wait_send()

    for kind in (down_kind, up_kind):
        send_own(kind, lambda c: c.wait_send())

        @pl.loop(1, groups)
        def _(k):
            for a in range(half):
                settle(kind, k, a)


def body(
    sizes,
    attention_input,
    output_weight,
    adapter_down_weight,
    adapter_up_weight,
    fetched_local_numbers,
    request_adapter_entry,
):
    reps, groups, tps = sizes
    chips = tps // CORES
    rows, features = attention_input.shape
    stored, _, rank = adapter_down_weight.shape
    width = adapter_up_weight.shape[2]
    half = stored // reps
    held = half * rank
    tile = min(512, width)
    tiles = width // tile
    down = adapter_down_weight.transpose(0, 2, 1).reshape(reps, held, features)
    up = adapter_up_weight.reshape(reps, held, width)
    entry = jnp.broadcast_to(request_adapter_entry[:, None], (rows, held))
    any_space = pl.BlockSpec(memory_space=pl.ANY)
    vmem = pl.BlockSpec(memory_space=pltpu.VMEM)
    dma = pltpu.SemaphoreType.DMA
    f32, bf16 = jnp.float32, jnp.bfloat16
    return pl.pallas_call(
        functools.partial(kernel, (reps, groups, tps, rank)),
        out_shape=jax.ShapeDtypeStruct((rows, width), bf16),
        in_specs=[vmem, pl.BlockSpec(memory_space=pltpu.SMEM)] + [any_space] * 4,
        out_specs=vmem,
        scratch_shapes=[
            pltpu.VMEM((rows, features), bf16),
            pltpu.VMEM((tps, tiles, features, tile), bf16),
            pltpu.VMEM((groups, reps, held, features), bf16),
            pltpu.VMEM((groups, reps, held, width), bf16),
            pltpu.VMEM((tps, rows, width), f32),
            pltpu.VMEM((chips, rows, width), f32),
            pltpu.VMEM((max(chips - 1, 1), rows, width), f32),
            pltpu.VMEM((rows, held), f32),
            pltpu.VMEM((tps - 1, rows, held), f32),
            pltpu.VMEM((rows, held), jnp.int32),
            dma((3,)),
            dma((tps, tiles)),
            dma((2, chips)),
            dma((2, max(chips - 1, 1))),
            dma((2, tps - 1)),
            dma((3, groups, half)),
            dma((2, groups, half)),
            dma((3, groups, half)),
            dma((2, groups, half)),
        ],
        compiler_params=pltpu.CompilerParams(
            collective_id=0, has_side_effects=True, vmem_limit_bytes=56 * 1024 * 1024
        ),
    )(entry, fetched_local_numbers, attention_input, output_weight, down, up)


def solution(mesh):
    in_specs = (
        P(("rep", "dp"), "tp"),
        P("tp", None),
        P("dp", "tp", None),
        P("dp", None, "tp"),
        P("rep", None, None),
        P(("rep", "dp")),
    )
    out_specs = P(("rep", "dp"), "tp")
    sizes = (mesh.shape["rep"], mesh.shape["dp"], mesh.shape["tp"])
    return jax.shard_map(
        functools.partial(body, sizes),
        mesh=mesh,
        in_specs=in_specs,
        out_specs=out_specs,
        check_vma=False,
    )
```

time: 155 us -> 72.5 us (0.47)
  waiting for transfers between devices: 108 us -> 0 us
  Pallas kernels: 0 us -> 67.5 us
  matrix products: 14.5 us -> 0 us
  between operations: 13.4 us -> 0.01 us
  starting transfers between devices: 10 us -> 0 us
  other arithmetic: 3.67 us -> 0 us
    pallas_call x0 -> x1, Pallas kernels: none -> 67.5 us  [body(): pl.pallas_call(functools.partial(kernel, (reps, groups, tps, rank)), out_...]
    all_to_all x2 -> x0, waiting for transfers between devices: 58.6 us -> none  [the longest x1 48.2 us: body(): lax.all_to_all(outgoing_down, 'dp', split_axis=0, concat_axis=0, tiled=True)]
    reduce_scatter x1 -> x0, waiting for transfers between devices: 35.9 us -> none  [body(): lax.psum_scatter(partial_value, 'tp', scatter_dimension=1, tiled=True)]
    dot_general x3 -> x0, matrix products: 14.5 us -> none  [the longest x1 10.1 us: body(): jnp.dot(attention_input, output_weight, preferred_element_type=jnp.float32)]
    psum x1 -> x0, waiting for transfers between devices: 13.8 us -> none  [body(): reduced_activation = lax.psum(shrunk_part, 'tp')]
    all_to_all x2 -> x0, starting transfers between devices: 9.96 us -> none  [the longest x1 6.45 us: body(): lax.all_to_all(outgoing_down, 'dp', split_axis=0, concat_axis=0, tiled=True)]
    select_n x3 -> x0, other arithmetic: 2.77 us -> none  [the longest x2 1.6 us: body(): outgoing_down = jnp.take(adapter_down_weight, owner_source, axis=0)]
    gather x2 -> x0, local copies, waits for them, and re-layouts: 2.52 us -> none  [the longest x1 1.91 us: body(): outgoing_down = jnp.take(adapter_down_weight, owner_source, axis=0)]
  transfers between devices with their start and end apart: 4 -> 0, of which waited for: 4 -> 0; matrix products, arithmetic and copies ran while one was open for 8% -> 0% of each run, Pallas kernels for 0% -> 0%
where the time goes in v1:
time: 72.5 us; the launch traced here: 72.2 us
  Pallas kernels  67.5 us (93%)
  local copies, waits for them, and re-layouts  4.68 us (6%)
    pallas_call x1, Pallas kernels, body(): pl.pallas_call(functools.partial(kernel, (reps, groups, tps, rank)), out_...  67.5 us
    unnamed x2, local copies, waits for them, and re-layouts  3.24 us

profile of v1, /device:TPU:0, one launch (start us, length us, event | category | flops | bytes accessed | tf_op | source)
XLA Modules:
  0.0 72.2 jit_solution(1605688806884216102)
XLA Ops:
  0.0 1.4 %copy.7.fetched_ref = s32[4,4,2]{2,1,0:T(4,128)} copy(s32[4,4,2]{1,2,0:T(2,128)} %param.10) | data formatting | bytes 256 | tf_op args[4]
  1.4 1.4 %broadcast_in_dim.2.entry_ref = s32[256,128]{1,0:T(8,128)} broadcast(s32[256]{0:T(256)} %param.11), dimensions={0} | broadcast | bytes 132096 | tf_op jit(solution)/shard_map/broadcast_in_dim | solution.py:377
  2.8 67.5 %shard_map.64 = bf16[256,1024]{1,0:T(8,128)(2,1)} custom-call(s32[256,128]{1,0:T(8,128)} %broadcast_in_dim.2.entry_ref, s32[4,4,2]{2,1,0:T(4,128)} %copy.7.fetched_ref, bf16[256,2048]{1,0:T(8,128)(2,1)} %x_hbm.1, bf16[2048,4096]{1,0:T(8,128)(2,1)} %w_hbm.1, bf16[2,128,2048]{2,1,0:T(8,128)(2,1)} %bitcast.4, bf16[2,128,1024]{2,1,0:T(8,128)(2,1)} %bitcast.5), custom_call_target="tpu_custom_call" | custom-call | tf_op jit(solution)/shard_map/pallas_call | solution.py:382
  70.4 1.9 %copy.9 = bf16[256,1024]{1,0:T(8,128)(2,1)} copy(bf16[256,1024]{1,0:T(8,128)(2,1)} %shard_map.64) | data formatting | bytes 1048576

commit v2 on v1

v2 whole, which is shorter than its diff:
```python
import functools

import jax
import jax.numpy as jnp
from jax import lax
from jax.experimental import pallas as pl
from jax.experimental.pallas import tpu as pltpu
from jax.sharding import PartitionSpec as P

adapter_scale = 0.5
CORES = 2


def kernel(
    sizes,
    entry_ref,
    fetched_ref,
    x_hbm,
    w_hbm,
    down_hbm,
    up_hbm,
    out_ref,
    x,
    w,
    downs,
    ups,
    part,
    core_in,
    x_in,
    shr,
    shr_in,
    aid,
    place,
    row_out,
    row_in,
    code_out,
    code_in,
    ret_out,
    ret_in,
    local_sem,
    w_sem,
    core_sem,
    xs_sem,
    shr_sem,
    zd_sem,
    yd_sem,
    ed_sem,
    zu_sem,
    yu_sem,
    eu_sem,
    row_sem,
):
    reps, groups, tps, rank = sizes
    chips = tps // CORES
    rep = lax.axis_index("rep")
    me = lax.axis_index("dp")
    tp = lax.axis_index("tp")
    core = lax.rem(tp, CORES)
    chip = lax.div(tp, CORES)
    other_core = CORES * chip + (1 - core)
    other_rep = 1 - rep
    rows = x.shape[0]
    width = out_ref.shape[1]
    held = downs.shape[2]
    half = held // rank
    stored = half * reps
    cap = fetched_ref.shape[1]
    tiles, tile = w.shape[1], w.shape[3]
    last = groups - 1
    f32, bf16 = jnp.float32, jnp.bfloat16

    def remote(src, dst, send, recv, target):
        return pltpu.make_async_remote_copy(
            src_ref=src,
            dst_ref=dst,
            send_sem=send,
            recv_sem=recv,
            device_id=target,
            device_id_type=pl.DeviceIdType.MESH,
        )

    def start(c):
        c.start()

    def wait_send(c):
        c.wait_send()

    load_x = pltpu.make_async_copy(x_hbm, x, local_sem.at[0])
    load_down = pltpu.make_async_copy(down_hbm, downs.at[me], local_sem.at[1])
    load_up = pltpu.make_async_copy(up_hbm, ups.at[me], local_sem.at[2])
    load_x.start()

    def column_of(j):
        far = lax.rem(chip + lax.div(j, 2) + 1, chips)
        return CORES * far + jnp.where(lax.rem(j, 2) == 0, 1 - core, core)

    def load_w(j, n):
        first = pl.multiple_of(column_of(j) * width + n * tile, 128)
        return pltpu.make_async_copy(
            w_hbm.at[:, pl.ds(first, tile)], w.at[j, n], w_sem.at[j, n]
        )

    @pl.loop(0, tps)
    def _(j):
        for n in range(tiles):
            load_w(j, n).start()

    load_down.start()
    load_up.start()

    barrier = pltpu.get_barrier_semaphore()

    def greet(target):
        pl.semaphore_signal(
            barrier, inc=1, device_id=target, device_id_type=pl.DeviceIdType.MESH
        )

    @pl.when(me > 0)
    def _():
        greet({"dp": me - 1})

    @pl.when(me < last)
    def _():
        greet({"dp": me + 1})

    greet({"rep": other_rep})

    @pl.loop(1, tps)
    def _(q):
        greet({"tp": lax.rem(tp + q, tps)})

    edges = jnp.where(me > 0, 1, 0) + jnp.where(me < last, 1, 0)
    pl.semaphore_wait(barrier, tps + edges)

    down_kind = (downs, down_hbm, zd_sem, yd_sem, ed_sem)
    up_kind = (ups, up_hbm, zu_sem, yu_sem, eu_sem)
    at_end = (me == 0) | (me == last)
    serves = (me == 1) | (me == last - 1)
    step = (-1, 1)
    exists = (me > 0, me < last)
    next_inner = (me > 1, me < last - 1)

    def piece(a):
        return pl.ds(a * rank, rank)

    def z_copy(kind, owner, a, side, own=False):
        buffer, source, z = kind[:3]
        src = source.at[rep, piece(a)] if own else buffer.at[owner, rep, piece(a)]
        return remote(
            src,
            buffer.at[owner, rep, piece(a)],
            z.at[side, owner, a],
            z.at[2, owner, a],
            {"dp": me + step[side]},
        )

    def extra_copy(kind, owner, a, side):
        buffer, source, extra = kind[0], kind[1], kind[4]
        return remote(
            source.at[other_rep, piece(a)],
            buffer.at[owner, other_rep, piece(a)],
            extra.at[side, a],
            extra.at[3 - side, a],
            {"dp": me + step[side]},
        )

    def y_copy(kind, owner, a, mine):
        buffer, y = kind[0], kind[3]
        where = buffer.at[owner, rep if mine else other_rep, piece(a)]
        return remote(where, where, y.at[0, owner, a], y.at[1, owner, a], {"rep": other_rep})

    def own_to(kind, act, sides):
        for side in (0, 1):

            @pl.when(sides[side])
            def _():
                for a in range(half):
                    act(z_copy(kind, me, a, side, True))

    def extra_to(kind, act, sides):
        for side in (0, 1):

            @pl.when(sides[side])
            def _():
                for a in range(half):
                    act(extra_copy(kind, me, a, side))

    def each_owner(k, visit):
        for side in (0, 1):
            owner = me - step[side] * k

            @pl.when((owner >= 0) & (owner < groups))
            def _():
                visit(owner, side)

    def by_rows(k):
        return at_end & (k == 1)

    def by_extra(kind, owner, k):
        if kind is down_kind:
            return (k == 1) & ((owner == 0) | (owner == last))
        return (k == 1) & (owner > 0) & (owner < last) & (me > 0) & (me < last)

    def relay(kind, k, a, first):
        def visit(owner, side):
            def go():
                if first:
                    z_copy(kind, owner, a, side).wait_recv()

                @pl.when(exists[side])
                def _():
                    (start if first else wait_send)(z_copy(kind, owner, a, side))

                @pl.when(jnp.logical_not(by_extra(kind, owner, k)))
                def _():
                    (start if first else wait_send)(y_copy(kind, owner, a, True))

            if kind is down_kind:
                pl.when(jnp.logical_not(by_rows(k)))(go)
            else:
                go()

        each_owner(k, visit)

    def receive_other(kind, owner, side, k):
        extra = by_extra(kind, owner, k)

        @pl.when(extra)
        def _():
            for a in range(half):
                extra_copy(kind, owner, a, side).wait_recv()

        @pl.when(jnp.logical_not(extra))
        def _():
            for a in range(half):
                y_copy(kind, owner, a, False).wait_recv()

    down_first = next_inner
    up_first = (exists[0] & jnp.logical_not(next_inner[0]), exists[1] & jnp.logical_not(next_inner[1]))
    up_second = (next_inner[0] & jnp.logical_not(at_end), next_inner[1] & jnp.logical_not(at_end))
    up_third = (next_inner[0] & at_end, next_inner[1] & at_end)
    down_extra = (exists[0] & at_end, exists[1] & at_end)
    up_extra = up_second

    own_to(down_kind, start, down_first)
    own_to(up_kind, start, up_first)

    entry = jnp.broadcast_to(entry_ref[...].reshape(1, rows), (held, rows)).T
    aid[...] = jnp.zeros_like(aid)

    @pl.loop(0, groups)
    def _(o):
        number = aid[...]
        for e in range(cap):
            number = jnp.where(entry == cap * o + e, stored * o + fetched_ref[me, e, o], number)
        aid[...] = number

    lane = lax.broadcasted_iota(jnp.int32, (rows, held), 1)
    lane_adapter = lax.div(lane, rank)

    def chosen(o, h):
        return aid[...] == stored * o + half * h + lane_adapter

    load_x.wait()

    neighbour = jnp.where(me == 0, 1, last - 1)
    client = jnp.where(me == 1, 0, last)
    packed = row_out.shape[0]

    def row_copies():
        return (
            remote(row_out, row_in, row_sem.at[0], row_sem.at[1], {"dp": neighbour}),
            remote(code_out, code_in, row_sem.at[2], row_sem.at[3], {"dp": neighbour}),
        )

    ret_copy = remote(ret_out, ret_in, row_sem.at[4], row_sem.at[5], {"dp": client})

    @pl.when(at_end)
    def _():
        local = aid[...] - stored * neighbour
        uses = (local >= 0) & (local < stored)
        below = lax.broadcasted_iota(jnp.int32, (rows, rows), 1) < lax.broadcasted_iota(
            jnp.int32, (rows, rows), 0
        )
        order = jnp.dot(
            jnp.where(below, 1.0, 0.0).astype(bf16),
            jnp.where(uses, 1.0, 0.0).astype(bf16),
            preferred_element_type=f32,
        )
        spot = jnp.where(uses & (order == lane.astype(f32)), 1.0, 0.0)
        place[...] = spot.astype(bf16)
        pick = spot.T.astype(bf16)[:packed]
        row_out[...] = jnp.dot(pick, x[...], preferred_element_type=f32).astype(bf16)
        code_out[...] = jnp.dot(
            pick, local.astype(f32).astype(bf16), preferred_element_type=f32
        ).astype(bf16)
        for c in row_copies():
            c.start()

    def core_copy(s):
        return remote(
            part.at[2 * s], core_in.at[s], core_sem.at[0, s], core_sem.at[1, s], {"tp": other_core}
        )

    def chip_copy(s):
        far = lax.rem(chip + s + 1, chips)
        return remote(
            part.at[2 * s + 1],
            x_in.at[s],
            xs_sem.at[0, s],
            xs_sem.at[1, s],
            {"tp": CORES * far + core},
        )

    def multiply(j):
        @pl.loop(0, tiles)
        def _(n):
            load_w(j, n).wait()
            part[j, :, pl.ds(pl.multiple_of(n * tile, 128), tile)] = jnp.dot(
                x[...], w[j, n], preferred_element_type=f32
            )

    def pass_on(s):
        core_copy(s).wait_recv()
        part[2 * s + 1] = part[2 * s + 1] + core_in[s]
        chip_copy(s).start()

    @pl.loop(0, chips - 1)
    def _(s):
        multiply(2 * s)
        core_copy(s).start()

        @pl.when(s > 0)
        def _():
            pass_on(s - 1)

        multiply(2 * s + 1)

    pass_on(chips - 2)

    for a in range(half):
        relay(down_kind, 1, a, True)

    multiply(tps - 2)
    core_copy(chips - 1).start()
    multiply(tps - 1)

    def shrink(o, h):
        product = lax.dot_general(
            x[...], downs[o, h], (((1,), (1,)), ((), ())), preferred_element_type=f32
        )
        shr[...] += jnp.where(chosen(o, h), product, 0.0)

    shr[...] = jnp.zeros_like(shr)
    load_down.wait()

    def shrink_own(o, side):
        shrink(o, rep)

    @pl.loop(0, reps)
    def _(h):
        shrink(me, h)

    @pl.when(jnp.logical_not(at_end))
    def _():
        each_owner(1, shrink_own)

    for a in range(half):
        relay(down_kind, 2, a, True)
    own_to(up_kind, start, up_second)
    extra_to(down_kind, start, down_extra)
    each_owner(2, shrink_own)

    @pl.when(serves)
    def _():
        for c in row_copies():
            c.wait_recv()
        code = code_in[...].astype(f32).astype(jnp.int32)
        group = lax.div(lax.broadcasted_iota(jnp.int32, (packed, held), 1), rank)
        total = jnp.zeros((packed, held), f32)
        for h in range(reps):
            product = lax.dot_general(
                row_in[...], downs[me, h], (((1,), (1,)), ((), ())), preferred_element_type=f32
            )
            total = total + jnp.where(code == half * h + group, product, 0.0)
        ret_out[...] = total
        ret_copy.start()

    @pl.loop(3, groups)
    def _(k):
        for a in range(half):
            relay(down_kind, k, a, True)
        each_owner(k, shrink_own)

    own_to(up_kind, start, up_third)
    extra_to(up_kind, start, up_extra)

    for a in range(half):
        relay(up_kind, 1, a, True)

    @pl.loop(1, groups)
    def _(k):
        @pl.when(jnp.logical_not(by_rows(k)))
        def _():
            def visit(owner, side):
                receive_other(down_kind, owner, side, k)
                shrink(owner, other_rep)

            each_owner(k, visit)

    @pl.when(at_end)
    def _():
        ret_copy.wait_recv()
        rest = ret_in[...]
        spot = place[...][:, :packed]
        for _ in range(3):
            term = rest.astype(bf16)
            rest = rest - term.astype(f32)
            shr[...] += jnp.dot(spot, term, preferred_element_type=f32)

    def shr_copy(q):
        return remote(
            shr,
            shr_in.at[q - 1],
            shr_sem.at[0, q - 1],
            shr_sem.at[1, q - 1],
            {"tp": lax.rem(tp + q, tps)},
        )

    @pl.loop(1, tps)
    def _(q):
        shr_copy(q).start()

    for a in range(half):
        relay(up_kind, 2, a, True)

    base = part.at[tps - 1]
    core_copy(chips - 1).wait_recv()
    base[...] += core_in[chips - 1]

    @pl.loop(0, chips - 1)
    def _(s):
        chip_copy(s).wait_recv()
        base[...] += x_in[s]

    @pl.loop(3, groups)
    def _(k):
        for a in range(half):
            relay(up_kind, k, a, True)

    @pl.loop(1, tps)
    def _(q):
        shr_copy(q).wait()

    @pl.loop(1, tps)
    def _(q):
        shr[...] += shr_in[q - 1]

    def expand(o):
        factor = jnp.concatenate(
            [jnp.where(chosen(o, h), adapter_scale * shr[...], 0.0) for h in range(reps)], axis=1
        )
        high = factor.astype(bf16)
        low = (factor - high.astype(f32)).astype(bf16)
        up = ups[o].reshape(reps * held, width)
        base[...] += jnp.dot(high, up, preferred_element_type=f32) + jnp.dot(
            low, up, preferred_element_type=f32
        )

    load_up.wait()
    expand(me)

    @pl.loop(1, groups)
    def _(k):
        def visit(owner, side):
            receive_other(up_kind, owner, side, k)
            expand(owner)

        each_owner(k, visit)

    out_ref[...] = base[...].astype(out_ref.dtype)

    @pl.loop(0, chips)
    def _(s):
        core_copy(s).wait_send()

    @pl.loop(0, chips - 1)
    def _(s):
        chip_copy(s).wait_send()

    @pl.when(at_end)
    def _():
        for c in row_copies():
            c.wait_send()

    @pl.when(serves)
    def _():
        ret_copy.wait_send()

    own_to(down_kind, wait_send, down_first)
    extra_to(down_kind, wait_send, down_extra)
    own_to(up_kind, wait_send, exists)
    extra_to(up_kind, wait_send, up_extra)

    @pl.loop(1, groups)
    def _(k):
        for kind in (down_kind, up_kind):
            for a in range(half):
                relay(kind, k, a, False)


def body(
    sizes,
    attention_input,
    output_weight,
    adapter_down_weight,
    adapter_up_weight,
    fetched_local_numbers,
    request_adapter_entry,
):
    reps, groups, tps = sizes
    chips = tps // CORES
    rows, features = attention_input.shape
    stored, _, rank = adapter_down_weight.shape
    width = adapter_up_weight.shape[2]
    half = stored // reps
    held = half * rank
    tile = min(512, width)
    tiles = width // tile
    down = adapter_down_weight.transpose(0, 2, 1).reshape(reps, held, features)
    up = adapter_up_weight.reshape(reps, held, width)
    cap = fetched_local_numbers.shape[2]
    packed = rows * cap // groups
    any_space = pl.BlockSpec(memory_space=pl.ANY)
    vmem = pl.BlockSpec(memory_space=pltpu.VMEM)
    dma = pltpu.SemaphoreType.DMA
    f32, bf16 = jnp.float32, jnp.bfloat16
    return pl.pallas_call(
        functools.partial(kernel, (reps, groups, tps, rank)),
        out_shape=jax.ShapeDtypeStruct((rows, width), bf16),
        in_specs=[vmem, pl.BlockSpec(memory_space=pltpu.SMEM)] + [any_space] * 4,
        out_specs=vmem,
        scratch_shapes=[
            pltpu.VMEM((rows, features), bf16),
            pltpu.VMEM((tps, tiles, features, tile), bf16),
            pltpu.VMEM((groups, reps, held, features), bf16),
            pltpu.VMEM((groups, reps, held, width), bf16),
            pltpu.VMEM((tps, rows, width), f32),
            pltpu.VMEM((chips, rows, width), f32),
            pltpu.VMEM((max(chips - 1, 1), rows, width), f32),
            pltpu.VMEM((rows, held), f32),
            pltpu.VMEM((tps - 1, rows, held), f32),
            pltpu.VMEM((rows, held), jnp.int32),
            pltpu.VMEM((rows, held), bf16),
            pltpu.VMEM((packed, features), bf16),
            pltpu.VMEM((packed, features), bf16),
            pltpu.VMEM((packed, held), bf16),
            pltpu.VMEM((packed, held), bf16),
            pltpu.VMEM((packed, held), f32),
            pltpu.VMEM((packed, held), f32),
            dma((3,)),
            dma((tps, tiles)),
            dma((2, chips)),
            dma((2, max(chips - 1, 1))),
            dma((2, tps - 1)),
            dma((3, groups, half)),
            dma((2, groups, half)),
            dma((4, half)),
            dma((3, groups, half)),
            dma((2, groups, half)),
            dma((4, half)),
            dma((6,)),
        ],
        compiler_params=pltpu.CompilerParams(
            collective_id=0, has_side_effects=True, vmem_limit_bytes=56 * 1024 * 1024
        ),
    )(
        request_adapter_entry,
        fetched_local_numbers.transpose(0, 2, 1),
        attention_input,
        output_weight,
        down,
        up,
    )


def solution(mesh):
    in_specs = (
        P(("rep", "dp"), "tp"),
        P("tp", None),
        P("dp", "tp", None),
        P("dp", None, "tp"),
        P("rep", None, None),
        P(("rep", "dp")),
    )
    out_specs = P(("rep", "dp"), "tp")
    sizes = (mesh.shape["rep"], mesh.shape["dp"], mesh.shape["tp"])
    return jax.shard_map(
        functools.partial(body, sizes),
        mesh=mesh,
        in_specs=in_specs,
        out_specs=out_specs,
        check_vma=False,
    )
```

time: 72.5 us -> 65.6 us (0.905)
  Pallas kernels: 67.5 us -> 63.6 us
  local copies, waits for them, and re-layouts: 4.68 us -> 1.87 us
    pallas_call x1, Pallas kernels: 67.5 us -> 63.6 us  [body(): pl.pallas_call(functools.partial(kernel, (reps, groups, tps, rank)), out_...]
    broadcast_in_dim x1 -> x0, local copies, waits for them, and re-layouts: 1.43 us -> none  [body(): entry = jnp.broadcast_to(request_adapter_entry[:, None], (rows, held))]
    unnamed x2 -> x1, local copies, waits for them, and re-layouts: 3.24 us -> 1.87 us
where the time goes in v2:
time: 65.6 us; the launch traced here: 65.5 us
  Pallas kernels  63.6 us (97%)
  local copies, waits for them, and re-layouts  1.87 us (3%)
    pallas_call x1, Pallas kernels, body(): pl.pallas_call(functools.partial(kernel, (reps, groups, tps, rank)), out_...  63.6 us
    unnamed x1, local copies, waits for them, and re-layouts  1.87 us

profile of v2, /device:TPU:0, one launch (start us, length us, event | category | flops | bytes accessed | tf_op | source)
XLA Modules:
  0.0 65.5 jit_solution(14833614223779882344)
XLA Ops:
  0.0 63.6 %shard_map.64 = bf16[256,1024]{1,0:T(8,128)(2,1)} custom-call(s32[256]{0:T(256)} %entry_ref.1, s32[4,2,4]{2,1,0:T(2,128)} %bitcast.7, bf16[256,2048]{1,0:T(8,128)(2,1)} %x_hbm.1, bf16[2048,4096]{1,0:T(8,128)(2,1)} %w_hbm.1, bf16[2,128,2048]{2,1,0:T(8,128)(2,1)} %bitcast.5, bf16[2,128,1024]{2,1,0:T(8,128)(2,1)} %bitcast.6), custom_call_target="tpu_custom_call" | custom-call | tf_op jit(solution)/shard_map/pallas_call | solution.py:538
  63.6 1.9 %copy.8 = bf16[256,1024]{1,0:T(8,128)(2,1)} copy(bf16[256,1024]{1,0:T(8,128)(2,1)} %shard_map.64) | data formatting | bytes 1048576

commit v3 on v2

--- a/solution.py
+++ b/solution.py
@@ -169,12 +169,12 @@
         where = buffer.at[owner, rep if mine else other_rep, piece(a)]
         return remote(where, where, y.at[0, owner, a], y.at[1, owner, a], {"rep": other_rep})
 
-    def own_to(kind, act, sides):
+    def own_to(kind, act, sides, pieces=range(half)):
         for side in (0, 1):
 
             @pl.when(sides[side])
             def _():
-                for a in range(half):
+                for a in pieces:
                     act(z_copy(kind, me, a, side, True))
 
     def extra_to(kind, act, sides):
@@ -182,7 +182,7 @@
 
             @pl.when(sides[side])
             def _():
-                for a in range(half):
+                for a in extra_pieces(kind):
                     act(extra_copy(kind, me, a, side))
 
     def each_owner(k, visit):
@@ -196,7 +196,12 @@
     def by_rows(k):
         return at_end & (k == 1)
 
-    def by_extra(kind, owner, k):
+    def extra_pieces(kind):
+        return range(max(half // 2, 1)) if kind is down_kind else range(half)
+
+    def by_extra(kind, owner, k, a):
+        if a not in extra_pieces(kind):
+            return False
         if kind is down_kind:
             return (k == 1) & ((owner == 0) | (owner == last))
         return (k == 1) & (owner > 0) & (owner < last) & (me > 0) & (me < last)
@@ -211,7 +216,7 @@
                 def _():
                     (start if first else wait_send)(z_copy(kind, owner, a, side))
 
-                @pl.when(jnp.logical_not(by_extra(kind, owner, k)))
+                @pl.when(jnp.logical_not(by_extra(kind, owner, k, a)))
                 def _():
                     (start if first else wait_send)(y_copy(kind, owner, a, True))
 
@@ -223,16 +228,15 @@
         each_owner(k, visit)
 
     def receive_other(kind, owner, side, k):
-        extra = by_extra(kind, owner, k)
-
-        @pl.when(extra)
-        def _():
-            for a in range(half):
+        for a in range(half):
+            extra = by_extra(kind, owner, k, a)
+
+            @pl.when(extra)
+            def _():
                 extra_copy(kind, owner, a, side).wait_recv()
 
-        @pl.when(jnp.logical_not(extra))
-        def _():
-            for a in range(half):
+            @pl.when(jnp.logical_not(extra))
+            def _():
                 y_copy(kind, owner, a, False).wait_recv()
 
     down_first = next_inner
@@ -242,7 +246,8 @@
     down_extra = (exists[0] & at_end, exists[1] & at_end)
     up_extra = up_second
 
-    own_to(down_kind, start, down_first)
+    inner = jnp.logical_not(at_end)
+    own_to(down_kind, start, down_first, range(1))
     own_to(up_kind, start, up_first)
 
     entry = jnp.broadcast_to(entry_ref[...].reshape(1, rows), (held, rows)).T
@@ -274,6 +279,56 @@
         )
 
     ret_copy = remote(ret_out, ret_in, row_sem.at[4], row_sem.at[5], {"dp": client})
+
+    def core_copy(s):
+        return remote(
+            part.at[2 * s], core_in.at[s], core_sem.at[0, s], core_sem.at[1, s], {"tp": other_core}
+        )
+
+    def chip_copy(s):
+        far = lax.rem(chip + s + 1, chips)
+        return remote(
+            part.at[2 * s + 1],
+            x_in.at[s],
+            xs_sem.at[0, s],
+            xs_sem.at[1, s],
+            {"tp": CORES * far + core},
+        )
+
+    def multiply(j):
+        @pl.loop(0, tiles)
+        def _(n):
+            load_w(j, n).wait()
+            part[j, :, pl.ds(pl.multiple_of(n * tile, 128), tile)] = jnp.dot(
+                x[...], w[j, n], preferred_element_type=f32
+            )
+
+    def pass_on(s):
+        core_copy(s).wait_recv()
+        part[2 * s + 1] = part[2 * s + 1] + core_in[s]
+        chip_copy(s).start()
+
+    @pl.loop(0, chips - 1)
+    def _(s):
+        multiply(2 * s)
+        core_copy(s).start()
+
+        @pl.when(s > 0)
+        def _():
+            pass_on(s - 1)
+
+        multiply(2 * s + 1)
+
+    own_to(down_kind, start, down_first, range(1, half))
+    pass_on(chips - 2)
+
+    @pl.when(inner)
+    def _():
+        relay(down_kind, 1, 0, True)
+
+    multiply(tps - 2)
+    core_copy(chips - 1).start()
+    multiply(tps - 1)
 
     @pl.when(at_end)
     def _():
@@ -297,53 +352,15 @@
         for c in row_copies():
             c.start()
 
-    def core_copy(s):
-        return remote(
-            part.at[2 * s], core_in.at[s], core_sem.at[0, s], core_sem.at[1, s], {"tp": other_core}
-        )
-
-    def chip_copy(s):
-        far = lax.rem(chip + s + 1, chips)
-        return remote(
-            part.at[2 * s + 1],
-            x_in.at[s],
-            xs_sem.at[0, s],
-            xs_sem.at[1, s],
-            {"tp": CORES * far + core},
-        )
-
-    def multiply(j):
-        @pl.loop(0, tiles)
-        def _(n):
-            load_w(j, n).wait()
-            part[j, :, pl.ds(pl.multiple_of(n * tile, 128), tile)] = jnp.dot(
-                x[...], w[j, n], preferred_element_type=f32
-            )
-
-    def pass_on(s):
-        core_copy(s).wait_recv()
-        part[2 * s + 1] = part[2 * s + 1] + core_in[s]
-        chip_copy(s).start()
-
-    @pl.loop(0, chips - 1)
-    def _(s):
-        multiply(2 * s)
-        core_copy(s).start()
-
-        @pl.when(s > 0)
-        def _():
-            pass_on(s - 1)
-
-        multiply(2 * s + 1)
-
-    pass_on(chips - 2)
-
-    for a in range(half):
-        relay(down_kind, 1, a, True)
-
-    multiply(tps - 2)
-    core_copy(chips - 1).start()
-    multiply(tps - 1)
+    @pl.when(at_end)
+    def _():
+        for a in range(half):
+            relay(up_kind, 1, a, True)
+
+    @pl.when(inner)
+    def _():
+        for a in range(1, half):
+            relay(down_kind, 1, a, True)
 
     def shrink(o, h):
         product = lax.dot_general(
@@ -361,14 +378,15 @@
     def _(h):
         shrink(me, h)
 
-    @pl.when(jnp.logical_not(at_end))
+    @pl.when(inner)
     def _():
         each_owner(1, shrink_own)
 
-    for a in range(half):
+    relay(down_kind, 2, 0, True)
+    own_to(up_kind, start, up_second)
+    for a in range(1, half):
         relay(down_kind, 2, a, True)
-    own_to(up_kind, start, up_second)
-    extra_to(down_kind, start, down_extra)
+    own_to(up_kind, start, up_third)
     each_owner(2, shrink_own)
 
     @pl.when(serves)
@@ -390,26 +408,38 @@
     def _(k):
         for a in range(half):
             relay(down_kind, k, a, True)
+            if a == 0:
+
+                @pl.when(k == 3)
+                def _():
+                    extra_to(down_kind, start, down_extra)
+
         each_owner(k, shrink_own)
 
-    own_to(up_kind, start, up_third)
-    extra_to(up_kind, start, up_extra)
-
-    for a in range(half):
-        relay(up_kind, 1, a, True)
-
-    @pl.loop(1, groups)
-    def _(k):
-        @pl.when(jnp.logical_not(by_rows(k)))
-        def _():
-            def visit(owner, side):
+    def shrink_other(k, wanted):
+        def visit(owner, side):
+            def go():
                 receive_other(down_kind, owner, side, k)
                 shrink(owner, other_rep)
 
-            each_owner(k, visit)
+            pl.when(wanted(owner))(go)
+
+        each_owner(k, visit)
+
+    def from_end(owner):
+        return (owner == 0) | (owner == last)
+
+    @pl.when(inner)
+    def _():
+        shrink_other(1, lambda owner: jnp.logical_not(from_end(owner)))
+        for a in range(half):
+            relay(up_kind, 1, a, True)
+
+    extra_to(up_kind, start, up_extra)
 
     @pl.when(at_end)
     def _():
+        shrink_other(2, lambda owner: True)
         ret_copy.wait_recv()
         rest = ret_in[...]
         spot = place[...][:, :packed]
@@ -418,6 +448,18 @@
             rest = rest - term.astype(f32)
             shr[...] += jnp.dot(spot, term, preferred_element_type=f32)
 
+    for a in range(half):
+        relay(up_kind, 2, a, True)
+
+    @pl.when(inner)
+    def _():
+        shrink_other(2, lambda owner: True)
+        shrink_other(1, from_end)
+
+    @pl.loop(3, groups)
+    def _(k):
+        shrink_other(k, lambda owner: True)
+
     def shr_copy(q):
         return remote(
             shr,
@@ -430,9 +472,6 @@
     @pl.loop(1, tps)
     def _(q):
         shr_copy(q).start()
-
-    for a in range(half):
-        relay(up_kind, 2, a, True)
 
     base = part.at[tps - 1]
     core_copy(chips - 1).wait_recv()

time: 65.6 us -> 60.3 us (0.919)
  Pallas kernels: 63.6 us -> 58.2 us
    pallas_call x1, Pallas kernels: 63.6 us -> 58.2 us  [body(): pl.pallas_call(functools.partial(kernel, (reps, groups, tps, rank)), out_...]
where the time goes in v3:
time: 60.3 us; the launch traced here: 60.1 us
  Pallas kernels  58.2 us (97%)
  local copies, waits for them, and re-layouts  1.87 us (3%)
    pallas_call x1, Pallas kernels, body(): pl.pallas_call(functools.partial(kernel, (reps, groups, tps, rank)), out_...  58.2 us
    unnamed x1, local copies, waits for them, and re-layouts  1.87 us

profile of v3, /device:TPU:0, one launch (start us, length us, event | category | flops | bytes accessed | tf_op | source)
XLA Modules:
  0.0 60.1 jit_solution(8552244228405646493)
XLA Ops:
  0.0 58.2 %shard_map.64 = bf16[256,1024]{1,0:T(8,128)(2,1)} custom-call(s32[256]{0:T(256)} %entry_ref.1, s32[4,2,4]{2,1,0:T(2,128)} %bitcast.7, bf16[256,2048]{1,0:T(8,128)(2,1)} %x_hbm.1, bf16[2048,4096]{1,0:T(8,128)(2,1)} %w_hbm.1, bf16[2,128,2048]{2,1,0:T(8,128)(2,1)} %bitcast.5, bf16[2,128,1024]{2,1,0:T(8,128)(2,1)} %bitcast.6), custom_call_target="tpu_custom_call" | custom-call | tf_op jit(solution)/shard_map/pallas_call | solution.py:577
  58.2 1.9 %copy.8 = bf16[256,1024]{1,0:T(8,128)(2,1)} copy(bf16[256,1024]{1,0:T(8,128)(2,1)} %shard_map.64) | data formatting | bytes 1048576

commit v4 on v3

--- a/solution.py
+++ b/solution.py
@@ -28,7 +28,11 @@
     core_in,
     x_in,
     shr,
+    shr_own,
+    shr_core,
+    shr_pair,
     shr_in,
+    picked,
     aid,
     place,
     row_out,
@@ -89,6 +93,7 @@
     load_down = pltpu.make_async_copy(down_hbm, downs.at[me], local_sem.at[1])
     load_up = pltpu.make_async_copy(up_hbm, ups.at[me], local_sem.at[2])
     load_x.start()
+    load_up.start()
 
     def column_of(j):
         far = lax.rem(chip + lax.div(j, 2) + 1, chips)
@@ -106,7 +111,6 @@
             load_w(j, n).start()
 
     load_down.start()
-    load_up.start()
 
     barrier = pltpu.get_barrier_semaphore()
 
@@ -143,9 +147,9 @@
     def piece(a):
         return pl.ds(a * rank, rank)
 
-    def z_copy(kind, owner, a, side, own=False):
-        buffer, source, z = kind[:3]
-        src = source.at[rep, piece(a)] if own else buffer.at[owner, rep, piece(a)]
+    def z_copy(kind, owner, a, side, source=None):
+        buffer, _, z = kind[:3]
+        src = buffer.at[owner, rep, piece(a)] if source is None else source.at[piece(a)]
         return remote(
             src,
             buffer.at[owner, rep, piece(a)],
@@ -169,13 +173,13 @@
         where = buffer.at[owner, rep if mine else other_rep, piece(a)]
         return remote(where, where, y.at[0, owner, a], y.at[1, owner, a], {"rep": other_rep})
 
-    def own_to(kind, act, sides, pieces=range(half)):
+    def own_to(kind, act, sides, pieces=range(half), source=None):
         for side in (0, 1):
 
             @pl.when(sides[side])
             def _():
                 for a in pieces:
-                    act(z_copy(kind, me, a, side, True))
+                    act(z_copy(kind, me, a, side, kind[1].at[rep] if source is None else source))
 
     def extra_to(kind, act, sides):
         for side in (0, 1):
@@ -204,7 +208,7 @@
             return False
         if kind is down_kind:
             return (k == 1) & ((owner == 0) | (owner == last))
-        return (k == 1) & (owner > 0) & (owner < last) & (me > 0) & (me < last)
+        return (k == 1) & (me > 0) & (me < last)
 
     def relay(kind, k, a, first):
         def visit(owner, side):
@@ -216,7 +220,7 @@
                 def _():
                     (start if first else wait_send)(z_copy(kind, owner, a, side))
 
-                @pl.when(jnp.logical_not(by_extra(kind, owner, k, a)))
+                @pl.when(jnp.logical_not(by_extra(kind, owner, k, a) | by_rows(k)))
                 def _():
                     (start if first else wait_send)(y_copy(kind, owner, a, True))
 
@@ -244,11 +248,25 @@
     up_second = (next_inner[0] & jnp.logical_not(at_end), next_inner[1] & jnp.logical_not(at_end))
     up_third = (next_inner[0] & at_end, next_inner[1] & at_end)
     down_extra = (exists[0] & at_end, exists[1] & at_end)
-    up_extra = up_second
+    up_extra = next_inner
 
     inner = jnp.logical_not(at_end)
     own_to(down_kind, start, down_first, range(1))
-    own_to(up_kind, start, up_first)
+
+    neighbour = jnp.where(me == 0, 1, last - 1)
+    client = jnp.where(me == 1, 0, last)
+    load_up.wait()
+
+    @pl.when(serves)
+    def _():
+        for e in range(cap):
+            number = fetched_ref[client, e, me]
+            value = ups[me, 0, piece(0)]
+            for j in range(1, stored):
+                value = jnp.where(number == j, ups[me, j // half, piece(j % half)], value)
+            picked[piece(e)] = value
+
+    own_to(up_kind, start, up_first, source=picked)
 
     entry = jnp.broadcast_to(entry_ref[...].reshape(1, rows), (held, rows)).T
     aid[...] = jnp.zeros_like(aid)
@@ -268,8 +286,6 @@
 
     load_x.wait()
 
-    neighbour = jnp.where(me == 0, 1, last - 1)
-    client = jnp.where(me == 1, 0, last)
     packed = row_out.shape[0]
 
     def row_copies():
@@ -460,22 +476,45 @@
     def _(k):
         shrink_other(k, lambda owner: True)
 
-    def shr_copy(q):
+    block = rows // half
+    lane_group = lane_adapter[:block]
+
+    def spread(value):
+        total = value
+        for g in range(1, half):
+            total = total + pltpu.roll(value, g * rank, 1)
+        return total
+
+    whole = spread(shr[...])
+    pack = jnp.zeros((block, held), f32)
+    for g in range(half):
+        pack = jnp.where(lane_group == g, whole[g * block : (g + 1) * block], pack)
+    shr_own[...] = pack
+
+    shr_core_copy = remote(
+        shr_own, shr_core, shr_sem.at[0, chips - 1], shr_sem.at[1, chips - 1], {"tp": other_core}
+    )
+
+    def shr_copy(s):
+        far = lax.rem(chip + s + 1, chips)
         return remote(
-            shr,
-            shr_in.at[q - 1],
-            shr_sem.at[0, q - 1],
-            shr_sem.at[1, q - 1],
-            {"tp": lax.rem(tp + q, tps)},
-        )
-
-    @pl.loop(1, tps)
-    def _(q):
-        shr_copy(q).start()
-
+            shr_pair,
+            shr_in.at[s],
+            shr_sem.at[0, s],
+            shr_sem.at[1, s],
+            {"tp": CORES * far + core},
+        )
+
+    shr_core_copy.start()
     base = part.at[tps - 1]
     core_copy(chips - 1).wait_recv()
     base[...] += core_in[chips - 1]
+    shr_core_copy.wait_recv()
+    shr_pair[...] = shr_own[...] + shr_core[...]
+
+    @pl.loop(0, chips - 1)
+    def _(s):
+        shr_copy(s).start()
 
     @pl.loop(0, chips - 1)
     def _(s):
@@ -487,29 +526,45 @@
         for a in range(half):
             relay(up_kind, k, a, True)
 
-    @pl.loop(1, tps)
-    def _(q):
-        shr_copy(q).wait()
-
-    @pl.loop(1, tps)
-    def _(q):
-        shr[...] += shr_in[q - 1]
+    shr_own_sum = shr_pair[...]
+    for s in range(chips - 1):
+        shr_copy(s).wait_recv()
+        shr_own_sum = shr_own_sum + shr_in[s]
+    for g in range(half):
+        shr[g * block : (g + 1) * block] = spread(jnp.where(lane_group == g, shr_own_sum, 0.0))
 
     def expand(o):
+        masks = [chosen(o, h) for h in range(reps)]
+        expand_by(masks, ups[o].reshape(reps * held, width))
+
+    def expand_by(masks, up):
         factor = jnp.concatenate(
-            [jnp.where(chosen(o, h), adapter_scale * shr[...], 0.0) for h in range(reps)], axis=1
+            [jnp.where(mask, adapter_scale * shr[...], 0.0) for mask in masks], axis=1
         )
         high = factor.astype(bf16)
         low = (factor - high.astype(f32)).astype(bf16)
-        up = ups[o].reshape(reps * held, width)
         base[...] += jnp.dot(high, up, preferred_element_type=f32) + jnp.dot(
             low, up, preferred_element_type=f32
         )
 
-    load_up.wait()
     expand(me)
 
-    @pl.loop(1, groups)
+    @pl.when(at_end)
+    def _():
+        number = jnp.zeros((rows, held), jnp.int32)
+        for e in range(cap):
+            number = jnp.where(lane_adapter == e, fetched_ref[me, e, neighbour], number)
+        expand_by([aid[...] == stored * neighbour + number], ups[neighbour, rep])
+
+    @pl.when(inner)
+    def _():
+        def visit(owner, side):
+            receive_other(up_kind, owner, side, 1)
+            expand(owner)
+
+        each_owner(1, visit)
+
+    @pl.loop(2, groups)
     def _(k):
         def visit(owner, side):
             receive_other(up_kind, owner, side, k)
@@ -538,7 +593,15 @@
 
     own_to(down_kind, wait_send, down_first)
     extra_to(down_kind, wait_send, down_extra)
-    own_to(up_kind, wait_send, exists)
+    own_to(up_kind, wait_send, up_first, source=picked)
+    own_to(up_kind, wait_send, up_second)
+    own_to(up_kind, wait_send, up_third)
+    shr_core_copy.wait_send()
+
+    @pl.loop(0, chips - 1)
+    def _(s):
+        shr_copy(s).wait_send()
+
     extra_to(up_kind, wait_send, up_extra)
 
     @pl.loop(1, groups)
@@ -586,9 +649,13 @@
             pltpu.VMEM((groups, reps, held, width), bf16),
             pltpu.VMEM((tps, rows, width), f32),
             pltpu.VMEM((chips, rows, width), f32),
-            pltpu.VMEM((max(chips - 1, 1), rows, width), f32),
+            pltpu.VMEM((chips - 1, rows, width), f32),
             pltpu.VMEM((rows, held), f32),
-            pltpu.VMEM((tps - 1, rows, held), f32),
+            pltpu.VMEM((rows // half, held), f32),
+            pltpu.VMEM((rows // half, held), f32),
+            pltpu.VMEM((rows // half, held), f32),
+            pltpu.VMEM((chips - 1, rows // half, held), f32),
+            pltpu.VMEM((held, width), bf16),
             pltpu.VMEM((rows, held), jnp.int32),
             pltpu.VMEM((rows, held), bf16),
             pltpu.VMEM((packed, features), bf16),
@@ -600,8 +667,8 @@
             dma((3,)),
             dma((tps, tiles)),
             dma((2, chips)),
-            dma((2, max(chips - 1, 1))),
-            dma((2, tps - 1)),
+            dma((2, chips - 1)),
+            dma((2, chips)),
             dma((3, groups, half)),
             dma((2, groups, half)),
             dma((4, half)),

time: 60.3 us -> 60.4 us (level)
  no operation moved by 1% of the time
where the time goes in v4:
time: 60.4 us; the launch traced here: 60.2 us
  Pallas kernels  58.3 us (97%)
  local copies, waits for them, and re-layouts  1.87 us (3%)
    pallas_call x1, Pallas kernels, body(): pl.pallas_call(functools.partial(kernel, (reps, groups, tps, rank)), out_...  58.3 us
    unnamed x1, local copies, waits for them, and re-layouts  1.87 us

profile of v4, /device:TPU:0, one launch (start us, length us, event | category | flops | bytes accessed | tf_op | source)
XLA Modules:
  0.0 60.2 jit_solution(17284093331962271490)
XLA Ops:
  0.0 58.3 %shard_map.64 = bf16[256,1024]{1,0:T(8,128)(2,1)} custom-call(s32[256]{0:T(256)} %entry_ref.1, s32[4,2,4]{2,1,0:T(2,128)} %bitcast.7, bf16[256,2048]{1,0:T(8,128)(2,1)} %x_hbm.1, bf16[2048,4096]{1,0:T(8,128)(2,1)} %w_hbm.1, bf16[2,128,2048]{2,1,0:T(8,128)(2,1)} %bitcast.5, bf16[2,128,1024]{2,1,0:T(8,128)(2,1)} %bitcast.6), custom_call_target="tpu_custom_call" | custom-call | tf_op jit(solution)/shard_map/pallas_call | solution.py:640
  58.3 1.9 %copy.8 = bf16[256,1024]{1,0:T(8,128)(2,1)} copy(bf16[256,1024]{1,0:T(8,128)(2,1)} %shard_map.64) | data formatting | bytes 1048576

commit v5 on v4

--- a/solution.py
+++ b/solution.py
@@ -210,7 +210,13 @@
             return (k == 1) & ((owner == 0) | (owner == last))
         return (k == 1) & (me > 0) & (me < last)
 
-    def relay(kind, k, a, first):
+    def from_end(owner):
+        return (owner == 0) | (owner == last)
+
+    def not_from_end(owner):
+        return jnp.logical_not(from_end(owner))
+
+    def relay(kind, k, a, first, wanted=None):
         def visit(owner, side):
             def go():
                 if first:
@@ -224,7 +230,9 @@
                 def _():
                     (start if first else wait_send)(y_copy(kind, owner, a, True))
 
-            if kind is down_kind:
+            if wanted is not None:
+                pl.when(wanted(owner))(go)
+            elif kind is down_kind:
                 pl.when(jnp.logical_not(by_rows(k)))(go)
             else:
                 go()
@@ -335,13 +343,14 @@
 
         multiply(2 * s + 1)
 
+    pass_on(chips - 2)
     own_to(down_kind, start, down_first, range(1, half))
-    pass_on(chips - 2)
 
     @pl.when(inner)
     def _():
         relay(down_kind, 1, 0, True)
 
+    own_to(up_kind, start, up_third)
     multiply(tps - 2)
     core_copy(chips - 1).start()
     multiply(tps - 1)
@@ -402,8 +411,41 @@
     own_to(up_kind, start, up_second)
     for a in range(1, half):
         relay(down_kind, 2, a, True)
-    own_to(up_kind, start, up_third)
+
+    @pl.when(inner)
+    def _():
+        for a in range(half):
+            relay(up_kind, 1, a, True, from_end)
+
     each_owner(2, shrink_own)
+
+    @pl.loop(3, groups)
+    def _(k):
+        for a in range(half):
+            relay(down_kind, k, a, True)
+            if a == 0:
+
+                @pl.when(k == 3)
+                def _():
+                    extra_to(down_kind, start, down_extra)
+
+        each_owner(k, shrink_own)
+
+    def shrink_other(k, wanted):
+        def visit(owner, side):
+            def go():
+                receive_other(down_kind, owner, side, k)
+                shrink(owner, other_rep)
+
+            pl.when(wanted(owner))(go)
+
+        each_owner(k, visit)
+
+    @pl.when(inner)
+    def _():
+        shrink_other(1, not_from_end)
+        for a in range(half):
+            relay(up_kind, 1, a, True, not_from_end)
 
     @pl.when(serves)
     def _():
@@ -419,37 +461,6 @@
             total = total + jnp.where(code == half * h + group, product, 0.0)
         ret_out[...] = total
         ret_copy.start()
-
-    @pl.loop(3, groups)
-    def _(k):
-        for a in range(half):
-            relay(down_kind, k, a, True)
-            if a == 0:
-
-                @pl.when(k == 3)
-                def _():
-                    extra_to(down_kind, start, down_extra)
-
-        each_owner(k, shrink_own)
-
-    def shrink_other(k, wanted):
-        def visit(owner, side):
-            def go():
-                receive_other(down_kind, owner, side, k)
-                shrink(owner, other_rep)
-
-            pl.when(wanted(owner))(go)
-
-        each_owner(k, visit)
-
-    def from_end(owner):
-        return (owner == 0) | (owner == last)
-
-    @pl.when(inner)
-    def _():
-        shrink_other(1, lambda owner: jnp.logical_not(from_end(owner)))
-        for a in range(half):
-            relay(up_kind, 1, a, True)
 
     extra_to(up_kind, start, up_extra)
 
@@ -639,7 +650,7 @@
     f32, bf16 = jnp.float32, jnp.bfloat16
     return pl.pallas_call(
         functools.partial(kernel, (reps, groups, tps, rank)),
-        out_shape=jax.ShapeDtypeStruct((rows, width), bf16),
+        out_shape=pltpu.VMEM((rows, width), bf16),
         in_specs=[vmem, pl.BlockSpec(memory_space=pltpu.SMEM)] + [any_space] * 4,
         out_specs=vmem,
         scratch_shapes=[

time: 60.4 us -> 60 us (level)
  local copies, waits for them, and re-layouts: 1.87 us -> 0.8 us
  Pallas kernels: 58.3 us -> 59.1 us
    unnamed x1, local copies, waits for them, and re-layouts: 1.87 us -> 0.8 us
    pallas_call x1, Pallas kernels: 58.3 us -> 59.1 us  [body(): pl.pallas_call(functools.partial(kernel, (reps, groups, tps, rank)), out_...]
where the time goes in v5:
time: 60 us; the launch traced here: 59.9 us
  Pallas kernels  59.1 us (98%)
  local copies, waits for them, and re-layouts  0.8 us (1%)
    pallas_call x1, Pallas kernels, body(): pl.pallas_call(functools.partial(kernel, (reps, groups, tps, rank)), out_...  59.1 us

profile of v5, /device:TPU:0, one launch (start us, length us, event | category | flops | bytes accessed | tf_op | source)
XLA Modules:
  0.0 59.9 jit_solution(12157126948163773520)
XLA Ops:
  0.0 59.1 %shard_map.64 = bf16[256,1024]{1,0:T(8,128)(2,1)S(1)} custom-call(s32[256]{0:T(256)} %entry_ref.1, s32[4,2,4]{2,1,0:T(2,128)} %bitcast.7, bf16[256,2048]{1,0:T(8,128)(2,1)} %x_hbm.1, bf16[2048,4096]{1,0:T(8,128)(2,1)} %w_hbm.1, bf16[2,128,2048]{2,1,0:T(8,128)(2,1)} %bitcast.5, bf16[2,128,1024]{2,1,0:T(8,128)(2,1)} %bitcast.6), custom_call_target="tpu_custom_call" | custom-call | tf_op jit(solution)/shard_map/pallas_call | solution.py:651
  59.1 0.8 %copy.8 = bf16[256,1024]{1,0:T(8,128)(2,1)} copy(bf16[256,1024]{1,0:T(8,128)(2,1)S(1)} %shard_map.64) | data formatting | bytes 1048576

commit v6 on v5

--- a/solution.py
+++ b/solution.py
@@ -216,19 +216,24 @@
     def not_from_end(owner):
         return jnp.logical_not(from_end(owner))
 
-    def relay(kind, k, a, first, wanted=None):
+    def relay(kind, k, a, first, wanted=None, chained=False):
         def visit(owner, side):
             def go():
                 if first:
                     z_copy(kind, owner, a, side).wait_recv()
 
-                @pl.when(exists[side])
-                def _():
-                    (start if first else wait_send)(z_copy(kind, owner, a, side))
-
                 @pl.when(jnp.logical_not(by_extra(kind, owner, k, a) | by_rows(k)))
                 def _():
                     (start if first else wait_send)(y_copy(kind, owner, a, True))
+
+                left = jnp.logical_not(inner & (k == 1) & from_end(owner))
+                onward = exists[side] if first or a == half - 1 else exists[side] & left
+
+                @pl.when(onward)
+                def _():
+                    if chained:
+                        z_copy(kind, owner, a - 1, side).wait_send()
+                    (start if first else wait_send)(z_copy(kind, owner, a, side))
 
             if wanted is not None:
                 pl.when(wanted(owner))(go)
@@ -251,6 +256,7 @@
             def _():
                 y_copy(kind, owner, a, False).wait_recv()
 
+    inner = jnp.logical_not(at_end)
     down_first = next_inner
     up_first = (exists[0] & jnp.logical_not(next_inner[0]), exists[1] & jnp.logical_not(next_inner[1]))
     up_second = (next_inner[0] & jnp.logical_not(at_end), next_inner[1] & jnp.logical_not(at_end))
@@ -258,7 +264,6 @@
     down_extra = (exists[0] & at_end, exists[1] & at_end)
     up_extra = next_inner
 
-    inner = jnp.logical_not(at_end)
     own_to(down_kind, start, down_first, range(1))
 
     neighbour = jnp.where(me == 0, 1, last - 1)
@@ -348,12 +353,18 @@
 
     @pl.when(inner)
     def _():
-        relay(down_kind, 1, 0, True)
-
-    own_to(up_kind, start, up_third)
+        relay(down_kind, 1, 0, True, not_from_end)
+
     multiply(tps - 2)
     core_copy(chips - 1).start()
     multiply(tps - 1)
+
+    own_to(down_kind, wait_send, down_first, range(1, half))
+    own_to(up_kind, start, up_third)
+
+    @pl.when(inner)
+    def _():
+        relay(down_kind, 1, 0, True, from_end)
 
     @pl.when(at_end)
     def _():
@@ -374,9 +385,6 @@
         code_out[...] = jnp.dot(
             pick, local.astype(f32).astype(bf16), preferred_element_type=f32
         ).astype(bf16)
-        for c in row_copies():
-            c.start()
-
     @pl.when(at_end)
     def _():
         for a in range(half):
@@ -385,7 +393,8 @@
     @pl.when(inner)
     def _():
         for a in range(1, half):
-            relay(down_kind, 1, a, True)
+            relay(down_kind, 1, a, True, not_from_end)
+            relay(down_kind, 1, a, True, from_end, True)
 
     def shrink(o, h):
         product = lax.dot_general(
@@ -408,22 +417,23 @@
         each_owner(1, shrink_own)
 
     relay(down_kind, 2, 0, True)
-    own_to(up_kind, start, up_second)
+    own_to(up_kind, wait_send, up_third)
+
+    @pl.when(at_end)
+    def _():
+        for c in row_copies():
+            c.start()
+
     for a in range(1, half):
         relay(down_kind, 2, a, True)
-
-    @pl.when(inner)
-    def _():
-        for a in range(half):
-            relay(up_kind, 1, a, True, from_end)
-
+    own_to(up_kind, start, up_second)
     each_owner(2, shrink_own)
 
     @pl.loop(3, groups)
     def _(k):
         for a in range(half):
             relay(down_kind, k, a, True)
-            if a == 0:
+            if a == half - 1:
 
                 @pl.when(k == 3)
                 def _():
@@ -446,6 +456,9 @@
         shrink_other(1, not_from_end)
         for a in range(half):
             relay(up_kind, 1, a, True, not_from_end)
+        own_to(up_kind, wait_send, up_second)
+        for a in range(half):
+            relay(up_kind, 1, a, True, from_end, a > 0)
 
     @pl.when(serves)
     def _():
@@ -462,8 +475,6 @@
         ret_out[...] = total
         ret_copy.start()
 
-    extra_to(up_kind, start, up_extra)
-
     @pl.when(at_end)
     def _():
         shrink_other(2, lambda owner: True)
@@ -477,6 +488,7 @@
 
     for a in range(half):
         relay(up_kind, 2, a, True)
+    extra_to(up_kind, start, up_extra)
 
     @pl.when(inner)
     def _():
@@ -602,11 +614,9 @@
     def _():
         ret_copy.wait_send()
 
-    own_to(down_kind, wait_send, down_first)
+    own_to(down_kind, wait_send, down_first, range(1))
     extra_to(down_kind, wait_send, down_extra)
     own_to(up_kind, wait_send, up_first, source=picked)
-    own_to(up_kind, wait_send, up_second)
-    own_to(up_kind, wait_send, up_third)
     shr_core_copy.wait_send()
 
     @pl.loop(0, chips - 1)

time: 60 us -> 59.6 us (level)
  no operation moved by 1% of the time
where the time goes in v6:
time: 59.6 us; the launch traced here: 59.5 us
  Pallas kernels  58.6 us (98%)
  local copies, waits for them, and re-layouts  0.8 us (1%)
    pallas_call x1, Pallas kernels, body(): pl.pallas_call(functools.partial(kernel, (reps, groups, tps, rank)), out_...  58.6 us

profile of v6, /device:TPU:0, one launch (start us, length us, event | category | flops | bytes accessed | tf_op | source)
XLA Modules:
  0.0 59.5 jit_solution(8388838430187096039)
XLA Ops:
  0.0 58.6 %shard_map.64 = bf16[256,1024]{1,0:T(8,128)(2,1)S(1)} custom-call(s32[256]{0:T(256)} %entry_ref.1, s32[4,2,4]{2,1,0:T(2,128)} %bitcast.7, bf16[256,2048]{1,0:T(8,128)(2,1)} %x_hbm.1, bf16[2048,4096]{1,0:T(8,128)(2,1)} %w_hbm.1, bf16[2,128,2048]{2,1,0:T(8,128)(2,1)} %bitcast.5, bf16[2,128,1024]{2,1,0:T(8,128)(2,1)} %bitcast.6), custom_call_target="tpu_custom_call" | custom-call | tf_op jit(solution)/shard_map/pallas_call | solution.py:661
  58.7 0.8 %copy.8 = bf16[256,1024]{1,0:T(8,128)(2,1)} copy(bf16[256,1024]{1,0:T(8,128)(2,1)S(1)} %shard_map.64) | data formatting | bytes 1048576

commit v7 on v6

--- a/solution.py
+++ b/solution.py
@@ -451,15 +451,6 @@
 
         each_owner(k, visit)
 
-    @pl.when(inner)
-    def _():
-        shrink_other(1, not_from_end)
-        for a in range(half):
-            relay(up_kind, 1, a, True, not_from_end)
-        own_to(up_kind, wait_send, up_second)
-        for a in range(half):
-            relay(up_kind, 1, a, True, from_end, a > 0)
-
     @pl.when(serves)
     def _():
         for c in row_copies():
@@ -474,6 +465,15 @@
             total = total + jnp.where(code == half * h + group, product, 0.0)
         ret_out[...] = total
         ret_copy.start()
+
+    @pl.when(inner)
+    def _():
+        shrink_other(1, not_from_end)
+        for a in range(half):
+            relay(up_kind, 1, a, True, not_from_end)
+        own_to(up_kind, wait_send, up_second)
+        for a in range(half):
+            relay(up_kind, 1, a, True, from_end, a > 0)
 
     @pl.when(at_end)
     def _():

time: 59.6 us -> 58.2 us (0.977)
  Pallas kernels: 58.6 us -> 57.3 us
    pallas_call x1, Pallas kernels: 58.6 us -> 57.3 us  [body(): pl.pallas_call(functools.partial(kernel, (reps, groups, tps, rank)), out_...]
where the time goes in v7:
time: 58.2 us; the launch traced here: 58.1 us
  Pallas kernels  57.3 us (98%)
  local copies, waits for them, and re-layouts  0.8 us (1%)
    pallas_call x1, Pallas kernels, body(): pl.pallas_call(functools.partial(kernel, (reps, groups, tps, rank)), out_...  57.3 us

profile of v7, /device:TPU:0, one launch (start us, length us, event | category | flops | bytes accessed | tf_op | source)
XLA Modules:
  0.0 58.1 jit_solution(4727436504816971047)
XLA Ops:
  0.0 57.3 %shard_map.64 = bf16[256,1024]{1,0:T(8,128)(2,1)S(1)} custom-call(s32[256]{0:T(256)} %entry_ref.1, s32[4,2,4]{2,1,0:T(2,128)} %bitcast.7, bf16[256,2048]{1,0:T(8,128)(2,1)} %x_hbm.1, bf16[2048,4096]{1,0:T(8,128)(2,1)} %w_hbm.1, bf16[2,128,2048]{2,1,0:T(8,128)(2,1)} %bitcast.5, bf16[2,128,1024]{2,1,0:T(8,128)(2,1)} %bitcast.6), custom_call_target="tpu_custom_call" | custom-call | tf_op jit(solution)/shard_map/pallas_call | solution.py:661
  57.3 0.8 %copy.8 = bf16[256,1024]{1,0:T(8,128)(2,1)} copy(bf16[256,1024]{1,0:T(8,128)(2,1)S(1)} %shard_map.64) | data formatting | bytes 1048576

commit v8 on v7

--- a/solution.py
+++ b/solution.py
@@ -360,7 +360,6 @@
     multiply(tps - 1)
 
     own_to(down_kind, wait_send, down_first, range(1, half))
-    own_to(up_kind, start, up_third)
 
     @pl.when(inner)
     def _():
@@ -385,6 +384,9 @@
         code_out[...] = jnp.dot(
             pick, local.astype(f32).astype(bf16), preferred_element_type=f32
         ).astype(bf16)
+        for c in row_copies():
+            c.start()
+
     @pl.when(at_end)
     def _():
         for a in range(half):
@@ -417,15 +419,15 @@
         each_owner(1, shrink_own)
 
     relay(down_kind, 2, 0, True)
-    own_to(up_kind, wait_send, up_third)
-
-    @pl.when(at_end)
-    def _():
-        for c in row_copies():
-            c.start()
-
     for a in range(1, half):
         relay(down_kind, 2, a, True)
+
+    @pl.when(at_end)
+    def _():
+        for c in row_copies():
+            c.wait_send()
+
+    own_to(up_kind, start, up_third)
     own_to(up_kind, start, up_second)
     each_owner(2, shrink_own)
 
@@ -605,14 +607,11 @@
     def _(s):
         chip_copy(s).wait_send()
 
-    @pl.when(at_end)
-    def _():
-        for c in row_copies():
-            c.wait_send()
-
     @pl.when(serves)
     def _():
         ret_copy.wait_send()
+
+    own_to(up_kind, wait_send, up_third)
 
     own_to(down_kind, wait_send, down_first, range(1))
     extra_to(down_kind, wait_send, down_extra)

time: 58.2 us -> 58 us (level)
  no operation moved by 1% of the time
where the time goes in v8:
time: 58 us; the launch traced here: 57.8 us
  Pallas kernels  57 us (98%)
  local copies, waits for them, and re-layouts  0.8 us (1%)
    pallas_call x1, Pallas kernels, body(): pl.pallas_call(functools.partial(kernel, (reps, groups, tps, rank)), out_...  57 us

profile of v8, /device:TPU:0, one launch (start us, length us, event | category | flops | bytes accessed | tf_op | source)
XLA Modules:
  0.0 57.8 jit_solution(10461862065397466263)
XLA Ops:
  0.0 57.0 %shard_map.64 = bf16[256,1024]{1,0:T(8,128)(2,1)S(1)} custom-call(s32[256]{0:T(256)} %entry_ref.1, s32[4,2,4]{2,1,0:T(2,128)} %bitcast.7, bf16[256,2048]{1,0:T(8,128)(2,1)} %x_hbm.1, bf16[2048,4096]{1,0:T(8,128)(2,1)} %w_hbm.1, bf16[2,128,2048]{2,1,0:T(8,128)(2,1)} %bitcast.5, bf16[2,128,1024]{2,1,0:T(8,128)(2,1)} %bitcast.6), custom_call_target="tpu_custom_call" | custom-call | tf_op jit(solution)/shard_map/pallas_call | solution.py:660
  57.0 0.8 %copy.8 = bf16[256,1024]{1,0:T(8,128)(2,1)} copy(bf16[256,1024]{1,0:T(8,128)(2,1)S(1)} %shard_map.64) | data formatting | bytes 1048576
